TPU v7x, 32 devices: a whole 2x2x4 slice. The times are simulated.
32 devices in a mesh: depth: 4 (over x, core), tile: 8 (over z, y).
Axes of the slice: x: 2, y: 2, z: 4, core: 2. Of those that a mesh axis runs over, the one named last changes fastest.
Arguments:
- old_fields: float32 [2, 32, 512, 128], P(None, 'depth', 'tile'), may hold values from -6 to 6
- recv_block: int32 [4, 128], P('depth', 'tile'), may hold values from 0 to 511
- recv_count: int32 [4, 64], P('depth', 'tile'), may hold values from 0 to 2, as said below
- new_block: int32 [4, 128], P('depth', 'tile'), may hold values from 0 to 127
- moments: bfloat16 [4, 128, 4, 128, 128], P('depth', 'tile'), may hold values from -0.0606 to 0.0606, as said below
- new_volume: float32 [4, 1024, 128], P('depth', 'tile'), may hold values from 0.5 to 2
Outputs:
- new_fields: float32 [4, 1024, 2, 128], P('depth', 'tile')
Inputs may be any that keep to these rules, and one draw needn't show every extreme that they name: `recv_count`: the tiles of some quarter of each depth group hold 2 live slots from every source tile. `moments`: component 0 (intersection volumes) is nonnegative.
All inputs are finite; a program needn't handle non-finite values.
Results may differ from a plain program's by a relative error of at most 0.003.
Values may be sent and summed in bfloat16 or wider, within the bound.
A program may use at most 128 MiB of HBM per device.

v0:
```python
import jax
import jax.numpy as jnp
from jax import lax
from jax.sharding import PartitionSpec as P

CAP = 2


def with_halo(array, sides, width):
    for axis, dim in sides:
        size, length = (lax.axis_size(axis), array.shape[dim])
        up = [(i, (i + 1) % size) for i in range(size - 1)]
        down = [(j, i) for i, j in up]
        last = lax.slice_in_dim(array, length - width, length, axis=dim)
        initial = lax.slice_in_dim(array, 0, width, axis=dim)
        before = lax.ppermute(last, axis, up)
        after = lax.ppermute(initial, axis, down)
        array = jnp.concatenate([before, array, after], axis=dim)
    return array


def minmod(left_value, right_value):
    return (
        0.5
        * (jnp.sign(left_value) + jnp.sign(right_value))
        * jnp.minimum(jnp.abs(left_value), jnp.abs(right_value))
    )


def limited(centre, upper_side, lower_side):
    central = 0.5 * (upper_side - lower_side)
    return minmod(central, minmod(2.0 * (centre - lower_side), 2.0 * (upper_side - centre)))


def interior(offset, length, total):
    position = offset + jnp.arange(length, dtype=jnp.int32)
    return ((position > 0) & (position < total - 1)).astype(jnp.float32)


def per_device(old_fields, recv_block, recv_count, new_block, moments, new_volume):
    padded = with_halo(old_fields, (("depth", 1), ("tile", 2)), 1)
    centre = padded[:, 1:-1, 1:-1, :]
    layers = centre.shape[1]
    lateral = centre.shape[2]
    width_x = centre.shape[3]
    depth_keep = interior(lax.axis_index("depth") * layers, layers, layers * lax.axis_size("depth"))
    lateral_keep = interior(
        lax.axis_index("tile") * lateral, lateral, lateral * lax.axis_size("tile")
    )
    x_keep = interior(0, width_x, width_x)
    slope_depth = (
        limited(centre, padded[:, 2:, 1:-1, :], padded[:, :-2, 1:-1, :])
        * depth_keep[None, :, None, None]
    )
    slope_lateral = (
        limited(centre, padded[:, 1:-1, 2:, :], padded[:, 1:-1, :-2, :])
        * lateral_keep[None, None, :, None]
    )
    x_padded = jnp.pad(centre, ((0, 0), (0, 0), (0, 0), (1, 1)))
    slope_x = limited(centre, x_padded[..., 2:], x_padded[..., :-2]) * x_keep
    stacked = jnp.stack([centre, slope_depth, slope_lateral, slope_x], 0).transpose(2, 3, 0, 1, 4)
    blocks = stacked.reshape(layers * lateral, 8, width_x).astype(jnp.bfloat16)
    block_count = layers * lateral
    slot_count = recv_block.shape[1]
    source = jnp.arange(slot_count, dtype=jnp.int32) // CAP
    gathered = lax.all_gather(blocks, "tile", axis=0, tiled=True)
    fetched = gathered[source * block_count + recv_block[0]]
    alive_mask = (jnp.arange(slot_count, dtype=jnp.int32) % CAP < recv_count[0][source]).astype(
        jnp.float32
    )
    contribution = jnp.einsum(
        "jcno,jcfo->jfn",
        moments[0],
        fetched.reshape(slot_count, 4, 2, width_x),
        preferred_element_type=jnp.float32,
    )
    contribution = contribution * alive_mask[:, None, None]
    new_count = new_volume.shape[1]
    one_hot = (new_block[0][None, :] == jnp.arange(new_count, dtype=jnp.int32)[:, None]).astype(
        jnp.float32
    )
    summed = jnp.dot(
        one_hot, contribution.reshape(slot_count, 2 * width_x), precision=lax.Precision.HIGHEST
    )
    result = summed.reshape(new_count, 2, width_x) / new_volume[0][:, None, :]
    return result[None]


def solution(mesh):
    placed = (
        P(None, "depth", "tile", None),
        P("depth", "tile"),
        P("depth", "tile"),
        P("depth", "tile"),
        P("depth", "tile", None, None, None),
        P("depth", "tile", None),
    )
    return jax.shard_map(
        per_device,
        mesh=mesh,
        in_specs=placed,
        out_specs=P("depth", "tile", None, None),
        check_vma=False,
    )
```

profile of v0, /device:TPU:0, one launch (start us, length us, event | category | flops | bytes accessed | tf_op | source)
XLA Modules:
  0.0 171.6 jit_solution(12616896355087981375)
XLA Ops:
  6.5 0.0 copy-start
  6.5 0.0 copy-start.2
  6.5 0.0 all-gather.2.cloned.1.call-start
  6.5 1.0 fusion.26
  7.6 2.4 %collective-permute-start.1 = (f32[2,1,64,128]{3,2,1,0:T(8,128)S(1)}, f32[2,1,64,128]{3,2,1,0:T(8,128)S(1)}, u32[]{:S(2)}, u32[]{:S(2)}) collective-permute-start(f32[2,1,64,128]{3,2,1,0:T(8,128)S(1)} %get-tuple-element.12), channel_id=1, source_target_pairs={{0,8},{8,16},{16,24},{1,9},{9,17},{17,25},{2,10},{10,18},{18,26},{... | collective-permute-start | bytes 196616 | tf_op jit(solution)/shard_map/ppermute | solution.py:16
  9.9 1.3 collective-permute-start
  11.3 0.0 collective-permute-done.1
  11.3 3.9 %collective-permute-done = f32[2,1,64,128]{3,2,1,0:T(8,128)S(1)} collective-permute-done((f32[2,1,64,128]{3,2,1,0:T(8,128)S(1)}, f32[2,1,64,128]{3,2,1,0:T(8,128)S(1)}, u32[]{:S(2)}, u32[]{:S(2)}) %collective-permute-start) | collective-permute-done | bytes 65568 | tf_op jit(solution)/shard_map/ppermute | solution.py:17
  15.2 4.1 %convert_bitcast_fusion = (bf16[1,2,8,64,128]{4,3,2,1,0:T(8,128)(2,1)S(1)}, f32[2,10,64,128]{3,2,1,0:T(8,128)S(1)}, bf16[1,2,8,64,128]{4,3,2,1,0:T(8,128)(2,1)S(1)}, bf16[1,2,8,64,128]{4,3,2,1,0:T(8,128)(2,1)S(1)}) fusion(f32[2,8,64,128]{3,2,1,0:T(8,128)} %param.6, f32[2,10,64,128]{3,2,1,0:T(8,128)S(1)} %constant_dynamic-update-slice_fusion.2, ...), kind=kLoop, calls=%fused_computation.24 | loop fusion | flops 6684672 | bytes 1967104 | tf_op jit(solution)/shard_map/stack | solution.py:61
  19.3 1.3 collective-permute-start.2
  20.6 4.5 %collective-permute-start.3 = (f32[2,10,1,128]{3,2,1,0:T(1,128)S(1)}, f32[2,10,1,128]{3,2,1,0:T(1,128)S(1)}, u32[]{:S(2)}, u32[]{:S(2)}) collective-permute-start(f32[2,10,1,128]{3,2,1,0:T(1,128)S(1)} %get-tuple-element.6), channel_id=1, source_target_pairs={{0,1},{1,2},{2,3},{3,4},{4,5},{5,6},{6,7},{8,9},{9,10},{10,11},{11... | collective-permute-start | bytes 30728 | tf_op jit(solution)/shard_map/ppermute | solution.py:16
  25.2 0.0 collective-permute-done.2
  25.2 1.3 collective-permute-done.3
  26.5 0.0 copy-done.2
  26.6 0.9 fusion.16
  27.5 0.1 maximum_bitcast_fusion
  27.6 0.0 copy-start.1
  27.6 0.0 copy-start.4
  27.6 2.1 %copy.12 = bf16[8,64,4,2,128]{4,3,2,1,0:T(2,128)(2,1)} copy(bf16[8,64,4,2,128]{4,1,0,3,2:T(8,128)(2,1)S(1)} %maximum_bitcast_fusion) | data formatting | bytes 2097152 | tf_op jit(solution)/shard_map/convert_element_type | solution.py:62
  29.8 0.0 copy-start.3
  29.8 0.0 copy-start.5
  29.8 0.0 all-gather.2.cloned.1.call-update
  29.8 0.0 copy-done.1
  29.8 0.7 gather_fusion.1
  30.5 0.0 copy-done.4
  30.5 128.5 %all-gather.2.cloned.1.call-done = bf16[4096,8,128]{2,1,0:T(8,128)(2,1)} async-done(((bf16[512,8,128]{2,1,0:T(8,128)(2,1)}), bf16[4096,8,128]{2,1,0:T(8,128)(2,1)}) %all-gather.2.cloned.1.call-update) | async-done | bytes 8388624 | tf_op jit(solution)/shard_map/all_gather | solution.py:66
  159.0 4.0 %gather_fusion = bf16[16,8,128]{2,1,0:T(8,128)(2,1)S(1)} fusion(bf16[4096,8,128]{2,1,0:T(8,128)(2,1)} %all-gather.2.cloned.1.call-done, s32[1024]{0:T(1024)S(1)} %pad_clamp_fusion.1), kind=kCustom, calls=%fused_computation | custom fusion | bytes 65600 | tf_op jit(solution)/shard_map/gather | solution.py:67
  163.0 0.0 copy-done
  163.0 0.7 fusion.6
  163.6 0.0 copy-done.3
  163.7 0.0 copy-done.5
  163.7 0.3 fusion.2
  164.0 0.8 copy.14
  (11 shorter events, 0.1 us)
Async XLA Ops:
  6.5 156.5 %copy-start = (bf16[1,16,4,128,128]{4,3,2,1,0:T(8,128)(2,1)S(1)}, bf16[1,16,4,128,128]{4,3,2,1,0:T(8,128)(2,1)}, u32[]{:S(2)}) copy-start(bf16[1,16,4,128,128]{4,3,2,1,0:T(8,128)(2,1)} %param.10) | copy-start | bytes 6291460
  6.5 20.0 %copy-start.2 = (f32[2,8,64,128]{3,2,1,0:T(8,128)S(1)}, f32[2,8,64,128]{3,2,1,0:T(8,128)}, u32[]{:S(2)}) copy-start(f32[2,8,64,128]{3,2,1,0:T(8,128)} %param.6) | copy-start | bytes 1572868
  6.5 152.5 %all-gather.2.cloned.1.call-start = ((), (), s32[]{:S(2)}) async-start(), calls=%async_computation | async-start | bytes 9437184 | tf_op jit(solution)/shard_map/all_gather | solution.py:66
  7.6 3.7 %collective-permute-start.1 = (f32[2,1,64,128]{3,2,1,0:T(8,128)S(1)}, f32[2,1,64,128]{3,2,1,0:T(8,128)S(1)}, u32[]{:S(2)}, u32[]{:S(2)}) collective-permute-start(f32[2,1,64,128]{3,2,1,0:T(8,128)S(1)} %get-tuple-element.12), channel_id=1, source_target_pairs={{0,8},{8,16},{16,24},{1,9},{9,17},{17,25},{2,10},{10,18},{18,26},{... | collective-permute-start | bytes 196616 | tf_op jit(solution)/shard_map/ppermute | solution.py:16
  9.9 5.3 %collective-permute-start = (f32[2,1,64,128]{3,2,1,0:T(8,128)S(1)}, f32[2,1,64,128]{3,2,1,0:T(8,128)S(1)}, u32[]{:S(2)}, u32[]{:S(2)}) collective-permute-start(f32[2,1,64,128]{3,2,1,0:T(8,128)S(1)} %get-tuple-element.11), channel_id=1, source_target_pairs={{8,0},{16,8},{24,16},{9,1},{17,9},{25,17},{10,2},{18,10},{26,18},{... | collective-permute-start | bytes 196616 | tf_op jit(solution)/shard_map/ppermute | solution.py:17
  19.3 5.9 %collective-permute-start.2 = (f32[2,10,1,128]{3,2,1,0:T(1,128)S(1)}, f32[2,10,1,128]{3,2,1,0:T(1,128)S(1)}, u32[]{:S(2)}, u32[]{:S(2)}) collective-permute-start(f32[2,10,1,128]{3,2,1,0:T(1,128)S(1)} %get-tuple-element.5), channel_id=1, source_target_pairs={{1,0},{2,1},{3,2},{4,3},{5,4},{6,5},{7,6},{9,8},{10,9},{11,10},{12... | collective-permute-start | bytes 30728 | tf_op jit(solution)/shard_map/ppermute | solution.py:17
  20.6 5.9 %collective-permute-start.3 = (f32[2,10,1,128]{3,2,1,0:T(1,128)S(1)}, f32[2,10,1,128]{3,2,1,0:T(1,128)S(1)}, u32[]{:S(2)}, u32[]{:S(2)}) collective-permute-start(f32[2,10,1,128]{3,2,1,0:T(1,128)S(1)} %get-tuple-element.6), channel_id=1, source_target_pairs={{0,1},{1,2},{2,3},{3,4},{4,5},{5,6},{6,7},{8,9},{9,10},{10,11},{11... | collective-permute-start | bytes 30728 | tf_op jit(solution)/shard_map/ppermute | solution.py:16
  27.6 2.2 %copy-start.1 = (s32[1,8]{1,0:T(1,128)S(1)}, s32[1,8]{1,0:T(1,128)}, u32[]{:S(2)}) copy-start(s32[1,8]{1,0:T(1,128)} %param.8) | copy-start | bytes 100
  27.6 2.9 %copy-start.4 = (s32[1,16]{1,0:T(1,128)S(1)}, s32[1,16]{1,0:T(1,128)}, u32[]{:S(2)}) copy-start(s32[1,16]{1,0:T(1,128)} %param.7) | copy-start | bytes 196
  29.8 133.9 %copy-start.3 = (f32[1,128,128]{2,1,0:T(8,128)S(1)}, f32[1,128,128]{2,1,0:T(8,128)}, u32[]{:S(2)}) copy-start(f32[1,128,128]{2,1,0:T(8,128)} %param.11) | copy-start | bytes 196612
  29.8 133.9 %copy-start.5 = (s32[1,16]{1,0:T(1,128)S(1)}, s32[1,16]{1,0:T(1,128)}, u32[]{:S(2)}) copy-start(s32[1,16]{1,0:T(1,128)} %param.9) | copy-start | bytes 196
Sparse Core Ops, SparseCore 0:
  29.9 129.0 all-gather.1
where the time goes:
time: 172 us
  waiting for transfers between devices  134 us (78%)
  between operations  13.6 us (8%)
  starting transfers between devices  9.49 us (6%)
  local copies, waits for them, and re-layouts  8.61 us (5%)
  other arithmetic  5.17 us (3%)
    all_gather x1, waiting for transfers between devices, per_device(): gathered = lax.all_gather(blocks, 'tile', axis=0, tiled=True)  128 us
    ppermute x2, starting transfers between devices, with_halo(): before = lax.ppermute(last, axis, up)  6.91 us
    another operation x2, other arithmetic, per_device(): jnp.stack([centre, slope_depth, slope_lateral, slope_x], 0)  4.98 us
    gather x1, local copies, waits for them, and re-layouts, per_device(): fetched = gathered[source * block_count + recv_block[0]]  3.96 us
    ppermute x2, waiting for transfers between devices, with_halo(): after = lax.ppermute(initial, axis, down)  3.9 us
  transfers between devices with their start and end apart: 5, of which 3 were waited for; matrix products, arithmetic and copies ran while one was open for 0% of the time, Pallas kernels for 0%

commit v1 on v0

--- a/solution.py
+++ b/solution.py
@@ -63,7 +63,12 @@
     block_count = layers * lateral
     slot_count = recv_block.shape[1]
     source = jnp.arange(slot_count, dtype=jnp.int32) // CAP
-    gathered = lax.all_gather(blocks, "tile", axis=0, tiled=True)
+    ring = [blocks]
+    for hop in range(7):
+        ring.append(lax.ppermute(ring[-1], "tile", [(dev, (dev + 1) % 8) for dev in range(8)]))
+    gathered = jnp.roll(
+        jnp.concatenate(ring[::-1], axis=0), (lax.axis_index("tile") + 1) * ring[0].shape[0], axis=0
+    )
     fetched = gathered[source * block_count + recv_block[0]]
     alive_mask = (jnp.arange(slot_count, dtype=jnp.int32) % CAP < recv_count[0][source]).astype(
         jnp.float32

time: 172 us -> 238 us (1.38)
  waiting for transfers between devices: 134 us -> 187 us
  local copies, waits for them, and re-layouts: 8.61 us -> 29.9 us
  between operations: 13.6 us -> 0.34 us
  starting transfers between devices: 9.49 us -> 12.1 us
    ppermute x0 -> x7, waiting for transfers between devices: none -> 182 us  [per_device(): lax.ppermute(ring[-1], 'tile', [(dev, (dev + 1) % 8) for dev in range(8)])]
    all_gather x1 -> x0, waiting for transfers between devices: 128 us -> none  [per_device(): gathered = lax.all_gather(blocks, 'tile', axis=0, tiled=True)]
    unnamed x13 -> x42, local copies, waits for them, and re-layouts: 0.03 us -> 18 us
    dynamic_slice x0 -> x1, local copies, waits for them, and re-layouts: none -> 3.65 us  [per_device(): jnp.roll(jnp.concatenate(ring[::-1], axis=0), (lax.axis_index('tile') + 1...]
    ppermute x0 -> x7, starting transfers between devices: none -> 2.62 us  [per_device(): lax.ppermute(ring[-1], 'tile', [(dev, (dev + 1) % 8) for dev in range(8)])]
  transfers between devices with their start and end apart: 5 -> 11, of which waited for: 3 -> 9; matrix products, arithmetic and copies ran while one was open for 0% -> 1% of each run, Pallas kernels for 0% -> 0%
where the time goes in v1:
time: 238 us; the launch traced here: 237 us
  waiting for transfers between devices  187 us (79%)
  local copies, waits for them, and re-layouts  29.9 us (13%)
  starting transfers between devices  12.1 us (5%)
  other arithmetic  6.72 us (3%)
    ppermute x7, waiting for transfers between devices, per_device(): lax.ppermute(ring[-1], 'tile', [(dev, (dev + 1) % 8) for dev in range(8)])  182 us
    unnamed x42, local copies, waits for them, and re-layouts  18 us
    ppermute x2, starting transfers between devices, with_halo(): before = lax.ppermute(last, axis, up)  6.91 us
    another operation x2, other arithmetic, per_device(): jnp.stack([centre, slope_depth, slope_lateral, slope_x], 0)  5.88 us
  transfers between devices with their start and end apart: 11, of which 9 were waited for; matrix products, arithmetic and copies ran while one was open for 1% of the time, Pallas kernels for 0%

profile of v1, /device:TPU:0, one launch (start us, length us, event | category | flops | bytes accessed | tf_op | source)
XLA Modules:
  0.0 237.1 jit_solution(9773187749108028282)
XLA Ops:
  0.0 1.0 fusion.26
  1.0 2.4 collective-permute-start.1
  3.4 1.3 collective-permute-start
  4.8 3.9 %collective-permute-done = f32[2,1,64,128]{3,2,1,0:T(8,128)S(1)} collective-permute-done((f32[2,1,64,128]{3,2,1,0:T(8,128)S(1)}, f32[2,1,64,128]{3,2,1,0:T(8,128)S(1)}, u32[]{:S(2)}, u32[]{:S(2)}) %collective-permute-start) | collective-permute-done | bytes 65568 | tf_op jit(solution)/shard_map/ppermute | solution.py:17
  8.7 3.9 %convert_bitcast_fusion = (bf16[1,2,8,64,128]{4,3,2,1,0:T(8,128)(2,1)S(1)}, f32[2,10,64,128]{3,2,1,0:T(8,128)S(1)}, bf16[1,2,8,64,128]{4,3,2,1,0:T(8,128)(2,1)S(1)}, bf16[1,2,8,64,128]{4,3,2,1,0:T(8,128)(2,1)S(1)}) fusion(f32[2,8,64,128]{3,2,1,0:T(8,128)} %param.6, f32[2,10,64,128]{3,2,1,0:T(8,128)S(1)} %constant_dynamic-update-slice_fusion.2, ...), kind=kLoop, calls=%fused_computation.24 | loop fusion | flops 6684672 | bytes 1967104 | tf_op jit(solution)/shard_map/stack | solution.py:61
  12.6 1.3 collective-permute-start.2
  13.9 4.5 %collective-permute-start.3 = (f32[2,10,1,128]{3,2,1,0:T(1,128)S(1)}, f32[2,10,1,128]{3,2,1,0:T(1,128)S(1)}, u32[]{:S(2)}, u32[]{:S(2)}) collective-permute-start(f32[2,10,1,128]{3,2,1,0:T(1,128)S(1)} %get-tuple-element.6), channel_id=1, source_target_pairs={{0,1},{1,2},{2,3},{3,4},{4,5},{5,6},{6,7},{8,9},{9,10},{10,11},{11... | collective-permute-start | bytes 30728 | tf_op jit(solution)/shard_map/ppermute | solution.py:16
  18.5 1.3 collective-permute-done.3
  19.9 1.9 fusion.16
  21.8 0.1 maximum_bitcast_fusion
  22.0 1.1 copy.9
  23.0 2.5 %collective-permute-start.4 = (bf16[512,8,128]{2,1,0:T(8,128)(2,1)S(1)}, bf16[512,8,128]{2,1,0:T(8,128)(2,1)S(1)}, u32[]{:S(2)}, u32[]{:S(2)}) collective-permute-start(bf16[512,8,128]{2,1,0:T(8,128)(2,1)S(1)} %bitcast.55), channel_id=1, source_target_pairs={{0,1},{1,2},{2,3},{3,4},{4,5},{5,6},{6,7},{7,0},{8,9},{9,10},{10,1... | collective-permute-start | bytes 3145736 | tf_op jit(solution)/shard_map/ppermute | solution.py:68
  25.5 26.1 %collective-permute-done.4 = bf16[512,8,128]{2,1,0:T(8,128)(2,1)S(1)} collective-permute-done((bf16[512,8,128]{2,1,0:T(8,128)(2,1)S(1)}, bf16[512,8,128]{2,1,0:T(8,128)(2,1)S(1)}, u32[]{:S(2)}, u32[]{:S(2)}) %collective-permute-start.4) | collective-permute-done | bytes 1048608 | tf_op jit(solution)/shard_map/ppermute | solution.py:68
  51.6 1.0 copy-done.1
  52.7 0.1 collective-permute-start.5
  52.8 28.2 %collective-permute-done.5 = bf16[512,8,128]{2,1,0:T(8,128)(2,1)S(1)} collective-permute-done((bf16[512,8,128]{2,1,0:T(8,128)(2,1)S(1)}, bf16[512,8,128]{2,1,0:T(8,128)(2,1)S(1)}, u32[]{:S(2)}, u32[]{:S(2)}) %collective-permute-start.5) | collective-permute-done | bytes 1048608 | tf_op jit(solution)/shard_map/ppermute | solution.py:68
  81.0 0.9 copy-done.3
  82.0 27.6 %collective-permute-done.6 = bf16[512,8,128]{2,1,0:T(8,128)(2,1)S(1)} collective-permute-done((bf16[512,8,128]{2,1,0:T(8,128)(2,1)S(1)}, bf16[512,8,128]{2,1,0:T(8,128)(2,1)S(1)}, u32[]{:S(2)}, u32[]{:S(2)}) %collective-permute-start.6) | collective-permute-done | bytes 1048608 | tf_op jit(solution)/shard_map/ppermute | solution.py:68
  109.6 1.0 copy-done.5
  110.6 26.7 %collective-permute-done.7 = bf16[512,8,128]{2,1,0:T(8,128)(2,1)S(1)} collective-permute-done((bf16[512,8,128]{2,1,0:T(8,128)(2,1)S(1)}, bf16[512,8,128]{2,1,0:T(8,128)(2,1)S(1)}, u32[]{:S(2)}, u32[]{:S(2)}) %collective-permute-start.7) | collective-permute-done | bytes 1048608 | tf_op jit(solution)/shard_map/ppermute | solution.py:68
  137.3 1.0 copy-done.7
  138.3 25.8 %collective-permute-done.8 = bf16[512,8,128]{2,1,0:T(8,128)(2,1)S(1)} collective-permute-done((bf16[512,8,128]{2,1,0:T(8,128)(2,1)S(1)}, bf16[512,8,128]{2,1,0:T(8,128)(2,1)S(1)}, u32[]{:S(2)}, u32[]{:S(2)}) %collective-permute-start.8) | collective-permute-done | bytes 1048608 | tf_op jit(solution)/shard_map/ppermute | solution.py:68
  164.1 1.0 copy-done.9
  165.1 25.0 %collective-permute-done.9 = bf16[512,8,128]{2,1,0:T(8,128)(2,1)} collective-permute-done((bf16[512,8,128]{2,1,0:T(8,128)(2,1)S(1)}, bf16[512,8,128]{2,1,0:T(8,128)(2,1)}, u32[]{:S(2)}, u32[]{:S(2)}) %collective-permute-start.9) | collective-permute-done | bytes 1048608 | tf_op jit(solution)/shard_map/ppermute | solution.py:68
  190.1 0.7 fusion.23
  190.8 1.3 gather_fusion.1
  192.1 22.2 %collective-permute-done.10 = bf16[512,8,128]{2,1,0:T(8,128)(2,1)} collective-permute-done((bf16[512,8,128]{2,1,0:T(8,128)(2,1)}, bf16[512,8,128]{2,1,0:T(8,128)(2,1)}, u32[]{:S(2)}, u32[]{:S(2)}) %collective-permute-start.10) | collective-permute-done | bytes 1048608 | tf_op jit(solution)/shard_map/ppermute | solution.py:68
  214.4 1.3 constant_dynamic-update-slice_fusion.18
  215.7 1.4 constant_dynamic-update-slice_fusion.17
  217.0 1.4 constant_dynamic-update-slice_fusion.16
  218.4 1.4 constant_dynamic-update-slice_fusion.15
  219.8 1.4 constant_dynamic-update-slice_fusion.14
  221.1 1.4 constant_dynamic-update-slice_fusion.13
  222.5 1.4 constant_dynamic-update-slice_fusion.12
  223.9 0.1 constant_dynamic-update-slice_fusion.11
  224.0 1.4 constant_dynamic-update-slice_fusion.10
  225.4 1.4 constant_dynamic-update-slice_fusion.9
  226.8 0.1 constant_dynamic-update-slice_fusion.8
  226.9 0.1 constant_dynamic-update-slice_fusion.7
  227.1 0.1 constant_dynamic-update-slice_fusion.6
  227.3 0.1 constant_dynamic-update-slice_fusion.5
  227.4 0.1 constant_dynamic-update-slice_fusion.4
  227.6 0.1 constant_dynamic-update-slice_fusion.3
  227.7 3.6 %constant_dynamic-slice_fusion = bf16[4096,8,128]{2,1,0:T(8,128)(2,1)} fusion(bf16[8192,8,128]{2,1,0:T(8,128)(2,1)S(1)} %constant_dynamic-update-slice_fusion.3, s32[]{:T(128)S(6)} %select_n.62), kind=kLoop, calls=%fused_computation.69 | loop fusion | bytes 16777220 | tf_op jit(solution)/shard_map/jit(_roll_dynamic)/dynamic_slice | solution.py:69
  231.4 4.0 %gather_fusion = bf16[16,8,128]{2,1,0:T(8,128)(2,1)S(1)} fusion(bf16[4096,8,128]{2,1,0:T(8,128)(2,1)} %constant_dynamic-slice_fusion, s32[1024]{0:T(1024)S(1)} %get-tuple-element.14), kind=kCustom, calls=%fused_computation | custom fusion | bytes 65600 | tf_op jit(solution)/shard_map/gather | solution.py:72
  235.3 0.6 fusion.6
  236.0 0.3 fusion.2
  236.3 0.8 copy.11
  (37 shorter events, 0.1 us)
Async XLA Ops:
  0.0 235.3 %copy-start = (bf16[1,16,4,128,128]{4,3,2,1,0:T(8,128)(2,1)S(1)}, bf16[1,16,4,128,128]{4,3,2,1,0:T(8,128)(2,1)}, u32[]{:S(2)}) copy-start(bf16[1,16,4,128,128]{4,3,2,1,0:T(8,128)(2,1)} %param.10) | copy-start | bytes 6291460
  1.0 3.7 %collective-permute-start.1 = (f32[2,1,64,128]{3,2,1,0:T(8,128)S(1)}, f32[2,1,64,128]{3,2,1,0:T(8,128)S(1)}, u32[]{:S(2)}, u32[]{:S(2)}) collective-permute-start(f32[2,1,64,128]{3,2,1,0:T(8,128)S(1)} %get-tuple-element.12), channel_id=1, source_target_pairs={{0,8},{8,16},{16,24},{1,9},{9,17},{17,25},{2,10},{10,18},{18,26},{... | collective-permute-start | bytes 196616 | tf_op jit(solution)/shard_map/ppermute | solution.py:16
  3.4 5.3 %collective-permute-start = (f32[2,1,64,128]{3,2,1,0:T(8,128)S(1)}, f32[2,1,64,128]{3,2,1,0:T(8,128)S(1)}, u32[]{:S(2)}, u32[]{:S(2)}) collective-permute-start(f32[2,1,64,128]{3,2,1,0:T(8,128)S(1)} %get-tuple-element.11), channel_id=1, source_target_pairs={{8,0},{16,8},{24,16},{9,1},{17,9},{25,17},{10,2},{18,10},{26,18},{... | collective-permute-start | bytes 196616 | tf_op jit(solution)/shard_map/ppermute | solution.py:17
  12.6 5.9 %collective-permute-start.2 = (f32[2,10,1,128]{3,2,1,0:T(1,128)S(1)}, f32[2,10,1,128]{3,2,1,0:T(1,128)S(1)}, u32[]{:S(2)}, u32[]{:S(2)}) collective-permute-start(f32[2,10,1,128]{3,2,1,0:T(1,128)S(1)} %get-tuple-element.5), channel_id=1, source_target_pairs={{1,0},{2,1},{3,2},{4,3},{5,4},{6,5},{7,6},{9,8},{10,9},{11,10},{12... | collective-permute-start | bytes 30728 | tf_op jit(solution)/shard_map/ppermute | solution.py:17
  13.9 5.9 %collective-permute-start.3 = (f32[2,10,1,128]{3,2,1,0:T(1,128)S(1)}, f32[2,10,1,128]{3,2,1,0:T(1,128)S(1)}, u32[]{:S(2)}, u32[]{:S(2)}) collective-permute-start(f32[2,10,1,128]{3,2,1,0:T(1,128)S(1)} %get-tuple-element.6), channel_id=1, source_target_pairs={{0,1},{1,2},{2,3},{3,4},{4,5},{5,6},{6,7},{8,9},{9,10},{10,11},{11... | collective-permute-start | bytes 30728 | tf_op jit(solution)/shard_map/ppermute | solution.py:16
  23.0 28.6 %collective-permute-start.4 = (bf16[512,8,128]{2,1,0:T(8,128)(2,1)S(1)}, bf16[512,8,128]{2,1,0:T(8,128)(2,1)S(1)}, u32[]{:S(2)}, u32[]{:S(2)}) collective-permute-start(bf16[512,8,128]{2,1,0:T(8,128)(2,1)S(1)} %bitcast.55), channel_id=1, source_target_pairs={{0,1},{1,2},{2,3},{3,4},{4,5},{5,6},{6,7},{7,0},{8,9},{9,10},{10,1... | collective-permute-start | bytes 3145736 | tf_op jit(solution)/shard_map/ppermute | solution.py:68
  51.6 1.0 copy-start.1
  52.7 28.4 %collective-permute-start.5 = (bf16[512,8,128]{2,1,0:T(8,128)(2,1)S(1)}, bf16[512,8,128]{2,1,0:T(8,128)(2,1)S(1)}, u32[]{:S(2)}, u32[]{:S(2)}) collective-permute-start(bf16[512,8,128]{2,1,0:T(8,128)(2,1)S(1)} %collective-permute-done.4), channel_id=1, source_target_pairs={{0,1},{1,2},{2,3},{3,4},{4,5},{5,6},{6,7},{7,0},{8,9},{9,10},{10,1... | collective-permute-start | bytes 3145736 | tf_op jit(solution)/shard_map/ppermute | solution.py:68
  81.0 0.9 copy-start.3
  82.0 27.6 %collective-permute-start.6 = (bf16[512,8,128]{2,1,0:T(8,128)(2,1)S(1)}, bf16[512,8,128]{2,1,0:T(8,128)(2,1)S(1)}, u32[]{:S(2)}, u32[]{:S(2)}) collective-permute-start(bf16[512,8,128]{2,1,0:T(8,128)(2,1)S(1)} %collective-permute-done.5), channel_id=1, source_target_pairs={{0,1},{1,2},{2,3},{3,4},{4,5},{5,6},{6,7},{7,0},{8,9},{9,10},{10,1... | collective-permute-start | bytes 3145736 | tf_op jit(solution)/shard_map/ppermute | solution.py:68
  109.6 1.0 copy-start.5
  110.6 26.7 %collective-permute-start.7 = (bf16[512,8,128]{2,1,0:T(8,128)(2,1)S(1)}, bf16[512,8,128]{2,1,0:T(8,128)(2,1)S(1)}, u32[]{:S(2)}, u32[]{:S(2)}) collective-permute-start(bf16[512,8,128]{2,1,0:T(8,128)(2,1)S(1)} %collective-permute-done.6), channel_id=1, source_target_pairs={{0,1},{1,2},{2,3},{3,4},{4,5},{5,6},{6,7},{7,0},{8,9},{9,10},{10,1... | collective-permute-start | bytes 3145736 | tf_op jit(solution)/shard_map/ppermute | solution.py:68
  137.3 1.0 copy-start.7
  138.3 25.8 %collective-permute-start.8 = (bf16[512,8,128]{2,1,0:T(8,128)(2,1)S(1)}, bf16[512,8,128]{2,1,0:T(8,128)(2,1)S(1)}, u32[]{:S(2)}, u32[]{:S(2)}) collective-permute-start(bf16[512,8,128]{2,1,0:T(8,128)(2,1)S(1)} %collective-permute-done.7), channel_id=1, source_target_pairs={{0,1},{1,2},{2,3},{3,4},{4,5},{5,6},{6,7},{7,0},{8,9},{9,10},{10,1... | collective-permute-start | bytes 3145736 | tf_op jit(solution)/shard_map/ppermute | solution.py:68
  164.1 1.0 copy-start.9
  165.1 25.0 %collective-permute-start.9 = (bf16[512,8,128]{2,1,0:T(8,128)(2,1)S(1)}, bf16[512,8,128]{2,1,0:T(8,128)(2,1)}, u32[]{:S(2)}, u32[]{:S(2)}) collective-permute-start(bf16[512,8,128]{2,1,0:T(8,128)(2,1)S(1)} %collective-permute-done.8), channel_id=1, source_target_pairs={{0,1},{1,2},{2,3},{3,4},{4,5},{5,6},{6,7},{7,0},{8,9},{9,10},{10,1... | collective-permute-start | bytes 3145736 | tf_op jit(solution)/shard_map/ppermute | solution.py:68
  190.1 24.3 %collective-permute-start.10 = (bf16[512,8,128]{2,1,0:T(8,128)(2,1)}, bf16[512,8,128]{2,1,0:T(8,128)(2,1)}, u32[]{:S(2)}, u32[]{:S(2)}) collective-permute-start(bf16[512,8,128]{2,1,0:T(8,128)(2,1)} %collective-permute-done.9), channel_id=1, source_target_pairs={{0,1},{1,2},{2,3},{3,4},{4,5},{5,6},{6,7},{7,0},{8,9},{9,10},{10,1... | collective-permute-start | bytes 3145736 | tf_op jit(solution)/shard_map/ppermute | solution.py:68
  192.1 34.7 %copy-start.10 = (bf16[512,8,128]{2,1,0:T(8,128)(2,1)S(1)}, bf16[512,8,128]{2,1,0:T(8,128)(2,1)}, u32[]{:S(2)}) copy-start(bf16[512,8,128]{2,1,0:T(8,128)(2,1)} %copy-done.9) | copy-start | bytes 3145732
  192.1 34.8 %copy-start.8 = (bf16[512,8,128]{2,1,0:T(8,128)(2,1)S(1)}, bf16[512,8,128]{2,1,0:T(8,128)(2,1)}, u32[]{:S(2)}) copy-start(bf16[512,8,128]{2,1,0:T(8,128)(2,1)} %copy-done.7) | copy-start | bytes 3145732
  192.1 35.0 %copy-start.6 = (bf16[512,8,128]{2,1,0:T(8,128)(2,1)S(1)}, bf16[512,8,128]{2,1,0:T(8,128)(2,1)}, u32[]{:S(2)}) copy-start(bf16[512,8,128]{2,1,0:T(8,128)(2,1)} %copy-done.5) | copy-start | bytes 3145732
  192.1 35.1 %copy-start.4 = (bf16[512,8,128]{2,1,0:T(8,128)(2,1)S(1)}, bf16[512,8,128]{2,1,0:T(8,128)(2,1)}, u32[]{:S(2)}) copy-start(bf16[512,8,128]{2,1,0:T(8,128)(2,1)} %copy-done.3) | copy-start | bytes 3145732
  192.1 35.3 %copy-start.2 = (bf16[512,8,128]{2,1,0:T(8,128)(2,1)S(1)}, bf16[512,8,128]{2,1,0:T(8,128)(2,1)}, u32[]{:S(2)}) copy-start(bf16[512,8,128]{2,1,0:T(8,128)(2,1)} %copy-done.1) | copy-start | bytes 3145732
  225.4 10.6 %copy-start.11 = (f32[1,128,128]{2,1,0:T(8,128)S(1)}, f32[1,128,128]{2,1,0:T(8,128)}, u32[]{:S(2)}) copy-start(f32[1,128,128]{2,1,0:T(8,128)} %param.11) | copy-start | bytes 196612
  225.4 10.6 %copy-start.12 = (s32[1,16]{1,0:T(1,128)S(1)}, s32[1,16]{1,0:T(1,128)}, u32[]{:S(2)}) copy-start(s32[1,16]{1,0:T(1,128)} %param.9) | copy-start | bytes 196
